TPU v7x, 256 devices: a whole 4x4x8 slice. The times are simulated.
256 devices in a mesh: store: 32 (over z, y), pb: 8 (over x, core).
Axes of the slice: x: 4, y: 4, z: 8, core: 2. Of those that a mesh axis runs over, the one named last changes fastest.
Arguments:
- stored_hidden: bfloat16 [640, 32, 4096], P('store')
- targets: int32 [640, 32], P('store'), may hold values from 0 to 5119
- pick: int32 [512], P('store'), may hold values from 0 to 19, as said below
- dest: int32 [512], P('store'), may hold values from 0 to 31, as said below
- norm_gain: float32 [4096], replicated, may hold values from 0.1 to 1.9
- head: bfloat16 [4096, 5120], P(None, 'pb')
- proj_in: bfloat16 [4096, 64], replicated, may hold values from -0.09375 to 0.09375
- proj_out: bfloat16 [5120, 128], P('pb'), may hold values from -6 to 6
- query_grads: bfloat16 [4096, 8192], P(('store', 'pb')), may hold values from -0.011962891 to 0.011962891
Outputs:
- shortlist: float32 [4096, 2], P(('store', 'pb'))
Inputs may be any that keep to these rules, and one draw needn't show every extreme that they name: `pick`: within one storage shard's 16 candidates the example numbers are distinct. `dest`: one storage shard sends at most 2 candidates to one query block; every query block receives at least 2 candidates.
All inputs are finite; a program needn't handle non-finite values.
Results may differ from a plain program's by a relative error of at most 0.003.
Values may be sent and summed in bfloat16 or wider, within the bound.
A program may use at most 128 MiB of HBM per device.

v0:
```python
import jax
import jax.numpy as jnp
from jax import lax
from jax.sharding import PartitionSpec as P

CAP = 2
K_TOP = 2


def combined_all(part, axis, combine):
    gathered = jax.tree.map(lambda a: lax.all_gather(a, axis), part)

    def take(source):
        return jax.tree.map(lambda a: lax.dynamic_index_in_dim(a, source, 0, False), gathered)

    return lax.fori_loop(
        1, lax.axis_size(axis), lambda source, state: combine(state, take(source)), take(0)
    )


def join_stats(first, second):
    top = jnp.maximum(first[0], second[0])
    total = first[1] * jnp.exp(first[0] - top) + second[1] * jnp.exp(second[0] - top)
    return (top, total)


def project_grads(hidden, wanted, norm_gain, head, proj_in, proj_out, pb_index):
    count = hidden.shape[0]
    tokens = hidden.shape[1]
    width = hidden.shape[2]
    v_dev = head.shape[1]
    flat = hidden.reshape(count * tokens, width)
    wide = flat.astype(jnp.float32)
    scale = lax.rsqrt(jnp.mean(wide * wide, axis=1) + 1e-05)
    normed = (wide * scale[:, None] * norm_gain[None, :]).astype(jnp.bfloat16)
    logits = jnp.dot(normed, head, preferred_element_type=jnp.float32)
    top_local = jnp.max(logits, axis=1)
    total_local = jnp.sum(jnp.exp(logits - top_local[:, None]), axis=1)
    top, total = combined_all((top_local, total_local), "pb", join_stats)
    prob = jnp.exp(logits - top[:, None]) / total[:, None]
    local_target = wanted.reshape(-1) - pb_index * v_dev
    hit = (jnp.arange(v_dev)[None, :] == local_target[:, None]).astype(jnp.float32)
    delta = (prob - hit).astype(jnp.bfloat16)
    outer_part = jnp.dot(delta, proj_out, preferred_element_type=jnp.float32)
    inner_side = jnp.dot(normed, proj_in, preferred_element_type=jnp.float32)
    outer_side = lax.psum(outer_part, "pb")
    inner_cube = inner_side.reshape(count, tokens, inner_side.shape[1])
    outer_cube = outer_side.reshape(count, tokens, outer_side.shape[1])
    grads = jnp.einsum("etk,etm->ekm", inner_cube, outer_cube, precision=lax.Precision.HIGHEST)
    return grads.reshape(count, inner_side.shape[1] * outer_side.shape[1]).astype(jnp.bfloat16)


def shards(stored_hidden, targets, pick, dest, norm_gain, head, proj_in, proj_out, query_grads):
    n_store = lax.axis_size("store")
    pb_index = lax.axis_index("pb")
    c_src = pick.shape[0]
    slots = n_store * CAP
    order = jnp.arange(c_src)
    same = dest[:, None] == dest[None, :]
    rank = jnp.sum(same & (order[:, None] < order[None, :]), axis=0)
    slot_of = dest * CAP + rank
    match = jnp.arange(slots)[:, None] == slot_of[None, :]
    live = jnp.any(match, axis=1)
    example = jnp.sum(jnp.where(match, pick[None, :], 0), axis=1)
    live_flag = live.astype(jnp.int32)
    rows = jnp.take(stored_hidden, example, axis=0)
    rows = jnp.where(live[:, None, None], rows, jnp.zeros_like(rows))
    sent_targets = jnp.where(live[:, None], jnp.take(targets, example, axis=0), 0)
    hidden, got_targets, got_live = (
        lax.all_to_all(rows, "store", split_axis=0, concat_axis=0, tiled=True),
        lax.all_to_all(sent_targets, "store", split_axis=0, concat_axis=0, tiled=True),
        lax.all_to_all(live_flag, "store", split_axis=0, concat_axis=0, tiled=True),
    )
    grads = project_grads(hidden, got_targets, norm_gain, head, proj_in, proj_out, pb_index)
    scores = lax.dot_general(
        query_grads, grads, (((1,), (1,)), ((), ())), preferred_element_type=jnp.float32
    )
    masked = jnp.where(got_live[None, :] > 0, scores, jnp.float32(-1e30))
    return lax.top_k(masked, K_TOP)[0]


def solution(mesh):
    placed = (
        P("store", None, None),
        P("store", None),
        P("store"),
        P("store"),
        P(),
        P(None, "pb"),
        P(),
        P("pb", None),
        P(("store", "pb"), None),
    )
    return jax.shard_map(
        shards, mesh=mesh, in_specs=placed, out_specs=P(("store", "pb"), None), check_vma=False
    )
```

profile of v0, /device:TPU:1, one launch (start us, length us, event | category | flops | bytes accessed | tf_op | source)
XLA Modules:
  0.0 625.4 jit_solution(8937116035219722497)
XLA Ops:
  6.5 0.0 copy-start
  6.5 0.8 convert_reduce_fusion
  7.4 0.7 multiply_add_fusion.1
  8.0 0.1 fusion.11
  8.1 0.7 reshape.107
  8.8 12.0 %all-to-all-start = ((s32[32,2,1]{1,2,0:T(1,128)}), s32[32,2,1]{1,2,0:T(1,128)S(1)}, u32[]{:S(2)}, u32[]{:S(2)}) async-start(s32[32,2,1]{1,2,0:T(1,128)} %bitcast.2), calls=%async_computation | async-start | bytes 32768 | tf_op jit(solution)/shard_map/all_to_all | solution.py:72
  20.9 0.7 select_reduce_fusion
  21.6 0.1 reduce_sum.45
  21.7 0.1 broadcast_in_dim.93
  21.9 1.3 gather_fusion.1
  23.2 0.7 select_select_fusion.1
  23.9 9.8 %gather_fusion = bf16[64,32,4096]{2,1,0:T(8,128)(2,1)} fusion(bf16[20,32,4096]{2,1,0:T(8,128)(2,1)} %param.11, s32[1024]{0:T(1024)S(1)} %pad_clamp_fusion), kind=kCustom, calls=%fused_computation | custom fusion | bytes 33554688 | tf_op jit(solution)/shard_map/jit(_take)/gather | solution.py:66
  33.7 0.0 all-to-all-done
  33.7 9.2 %all-to-all-start.2 = ((s32[32,2,32]{2,1,0:T(2,128)}), s32[32,2,32]{2,1,0:T(2,128)S(1)}, u32[]{:S(2)}, u32[]{:S(2)}) async-start(s32[32,2,32]{2,1,0:T(2,128)} %select_select_fusion.1), calls=%async_computation.2 | async-start | bytes 65536 | tf_op jit(solution)/shard_map/all_to_all | solution.py:71
  43.0 14.3 %select_select_fusion = bf16[64,32,4096]{2,1,0:T(8,128)(2,1)} fusion(bf16[64,32,4096]{2,1,0:T(8,128)(2,1)} %gather_fusion, pred[64]{0:T(512)(128)(4,1)S(1)} %compare_and_fusion.1, pred[64]{0:T(512)(128)(4,1)S(1)} %fusion.11), kind=kLoop, calls=%fused_computation.14 | loop fusion | flops 16777216 | bytes 33554560 | tf_op jit(solution)/shard_map/jit(_where)/select_n | solution.py:67
  57.3 0.0 all-to-all-done.2
  57.3 9.3 %all-to-all-start.1 = ((bf16[64,32,4096]{2,1,0:T(8,128)(2,1)}), bf16[64,32,4096]{2,1,0:T(8,128)(2,1)}, u32[]{:S(2)}, u32[]{:S(2)}) async-start(bf16[64,32,4096]{2,1,0:T(8,128)(2,1)} %select_select_fusion), calls=%async_computation.1 | async-start | bytes 33554432 | tf_op jit(solution)/shard_map/all_to_all | solution.py:70
  66.7 0.0 copy-start.1
  66.7 0.0 all-reduce.2.cloned.1.call-start
  66.7 0.1 compare_reduce_fusion
  66.8 0.1 gt.18
  66.9 0.1 sub.58
  67.0 383.3 %all-to-all-done.1 = bf16[64,32,4096]{2,1,0:T(8,128)(2,1)} async-done(((bf16[64,32,4096]{2,1,0:T(8,128)(2,1)}), bf16[64,32,4096]{2,1,0:T(8,128)(2,1)}, u32[]{:S(2)}, u32[]{:S(2)}) %all-to-all-start.1) | async-done | bytes 16777248 | tf_op jit(solution)/shard_map/all_to_all | solution.py:70
  450.3 7.2 %multiply_reduce_fusion = f32[64,32]{1,0:T(8,128)S(1)} fusion(bf16[64,32,4096]{2,1,0:T(8,128)(2,1)} %all-to-all-done.1), kind=kLoop, calls=%fused_computation.9 | loop fusion | flops 25163776 | bytes 16785408 | tf_op jit(solution)/shard_map/reduce_sum | solution.py:34
  457.5 0.1 rsqrt.12
  457.6 0.0 copy-done.1
  457.6 15.5 %fusion.1 = bf16[2048,4096]{1,0:T(8,128)(2,1)} fusion(f32[4096]{0:T(1024)S(1)} %copy-done.1, f32[2048]{0:T(1024)S(1)} %rsqrt.12, bf16[64,32,4096]{2,1,0:T(8,128)(2,1)} %all-to-all-done.1), kind=kLoop, calls=%fused_computation.7 | loop fusion | flops 33554432 | bytes 33579008 | tf_op jit(solution)/shard_map/convert_element_type | solution.py:35
  473.1 0.0 copy-start.3
  473.1 17.8 %fusion.14 = (f32[2048]{0:T(1024)S(1)}, f32[2048,640]{0,1:T(8,128)}) fusion(bf16[2048,4096]{1,0:T(8,128)(2,1)} %fusion.1, bf16[4096,640]{1,0:T(8,128)(2,1)} %param.16), kind=kOutput, calls=%fused_computation.43 | convolution fusion | flops 10738726912 | bytes 27271168 | tf_op jit(solution)/shard_map/dot_general | solution.py:36
  490.9 14.3 %all-gather = f32[16384]{0:T(1024)S(1)} all-gather(f32[2048]{0:T(1024)S(1)} %get-tuple-element.157), channel_id=2, replica_groups=mesh['store'=32,'pb'=8] {'pb'}, dimensions={0}, use_global_device_ids=true | all-gather | bytes 73728 | tf_op jit(solution)/shard_map/all_gather | solution.py:11
  505.2 3.2 exponential_reduce_fusion
  508.4 12.9 %all-gather.1 = f32[16384]{0:T(1024)S(1)} all-gather(f32[2048]{0:T(1024)S(1)} %exponential_reduce_fusion), channel_id=3, replica_groups=mesh['store'=32,'pb'=8] {'pb'}, dimensions={0}, use_global_device_ids=true | all-gather | bytes 73728 | tf_op jit(solution)/shard_map/all_gather | solution.py:11
  521.4 0.5 while.17
  521.8 0.0 copy-done.3
  521.8 5.1 fusion.6
  526.9 0.0 all-reduce.2.cloned.1.call-update
  527.0 0.0 copy-done
  527.0 0.0 copy-start.2
  527.0 8.3 %fusion.2 = f32[64,32,64]{2,1,0:T(8,128)S(1)} fusion(f32[4096]{0:T(1024)S(1)} %copy-done.1, f32[64,32]{1,0:T(8,128)S(1)} %add_rsqrt_fusion, bf16[64,32,4096]{2,1,0:T(8,128)(2,1)} %all-to-all-done.1, bf16[4096,64]{0,1:T(8,128)(2,1)S(1)} %copy-done), kind=kOutput, calls=%fused_computation.10 | convolution fusion | flops 1107296256 | bytes 17850368 | tf_op jit(solution)/shard_map/dot_general | solution.py:45
  535.3 75.8 %all-reduce.2.cloned.1.call-done = f32[64,32,128]{2,1,0:T(8,128)} async-done(((f32[64,32,128]{2,1,0:T(8,128)}), f32[64,32,128]{2,1,0:T(8,128)}) %all-reduce.2.cloned.1.call-update) | async-done | bytes 1048592 | tf_op jit(solution)/shard_map/psum | solution.py:46
  611.1 4.9 convolution_convert_fusion
  616.0 0.0 copy-done.2
  616.0 0.7 fusion.7
  616.7 0.1 copy.14
  616.8 1.1 top_k.9
  617.9 0.6 top_k.10
  (26 shorter events, 0.3 us)
Async XLA Ops:
  6.5 520.4 %copy-start = (bf16[4096,64]{0,1:T(8,128)(2,1)S(1)}, bf16[4096,64]{0,1:T(8,128)(2,1)}, u32[]{:S(2)}) copy-start(bf16[4096,64]{0,1:T(8,128)(2,1)} %param.17) | copy-start | bytes 1572868
  8.8 24.9 %all-to-all-start = ((s32[32,2,1]{1,2,0:T(1,128)}), s32[32,2,1]{1,2,0:T(1,128)S(1)}, u32[]{:S(2)}, u32[]{:S(2)}) async-start(s32[32,2,1]{1,2,0:T(1,128)} %bitcast.2), calls=%async_computation | async-start | bytes 32768 | tf_op jit(solution)/shard_map/all_to_all | solution.py:72
  33.7 23.6 %all-to-all-start.2 = ((s32[32,2,32]{2,1,0:T(2,128)}), s32[32,2,32]{2,1,0:T(2,128)S(1)}, u32[]{:S(2)}, u32[]{:S(2)}) async-start(s32[32,2,32]{2,1,0:T(2,128)} %select_select_fusion.1), calls=%async_computation.2 | async-start | bytes 65536 | tf_op jit(solution)/shard_map/all_to_all | solution.py:71
  57.3 393.0 %all-to-all-start.1 = ((bf16[64,32,4096]{2,1,0:T(8,128)(2,1)}), bf16[64,32,4096]{2,1,0:T(8,128)(2,1)}, u32[]{:S(2)}, u32[]{:S(2)}) async-start(bf16[64,32,4096]{2,1,0:T(8,128)(2,1)} %select_select_fusion), calls=%async_computation.1 | async-start | bytes 33554432 | tf_op jit(solution)/shard_map/all_to_all | solution.py:70
  66.7 390.9 %copy-start.1 = (f32[4096]{0:T(1024)S(1)}, f32[4096]{0:T(1024)}, u32[]{:S(2)}) copy-start(f32[4096]{0:T(1024)} %param.15) | copy-start | bytes 49156
  66.7 544.4 %all-reduce.2.cloned.1.call-start = ((), (), s32[]{:S(2)}) async-start(), calls=%async_computation.3 | async-start | bytes 2097152 | tf_op jit(solution)/shard_map/psum | solution.py:46
  473.1 48.8 %copy-start.3 = (bf16[640,128]{1,0:T(8,128)(2,1)S(1)}, bf16[640,128]{1,0:T(8,128)(2,1)}, u32[]{:S(2)}) copy-start(bf16[640,128]{1,0:T(8,128)(2,1)} %param.18) | copy-start | bytes 491524
  527.0 89.1 %copy-start.2 = (bf16[16,8192]{1,0:T(8,128)(2,1)S(1)}, bf16[16,8192]{1,0:T(8,128)(2,1)}, u32[]{:S(2)}) copy-start(bf16[16,8192]{1,0:T(8,128)(2,1)} %param.19) | copy-start | bytes 786436
Sparse Core Ops, SparseCore 0:
  527.1 83.9 all-reduce.1
where the time goes:
time: 627 us; the launch traced here: 625 us
  waiting for transfers between devices  459 us (73%)
  other arithmetic  44.6 us (7%)
  matrix products  36.8 us (6%)
  starting transfers between devices  30.7 us (5%)
  blocking collectives  27.2 us (4%)
  between operations  13.6 us (2%)
  local copies, waits for them, and re-layouts  13.1 us (2%)
    all_to_all x1, waiting for transfers between devices, shards(): lax.all_to_all(rows, 'store', split_axis=0, concat_axis=0, tiled=True)  383 us
    psum x1, waiting for transfers between devices, project_grads(): outer_side = lax.psum(outer_part, 'pb')  75.8 us
    all_gather x2, blocking collectives, combined_all(): gathered = jax.tree.map(lambda a: lax.all_gather(a, axis), part)  27.2 us
    dot_general x1, matrix products, project_grads(): logits = jnp.dot(normed, head, preferred_element_type=jnp.float32)  17.8 us
    convert_element_type x1, other arithmetic, project_grads(): normed = (wide * scale[:, None] * norm_gain[None, :]).astype(jnp.bfloat16)  15.5 us
    select_n x1, other arithmetic, shards(): rows = jnp.where(live[:, None, None], rows, jnp.zeros_like(rows))  14.3 us
  transfers between devices with their start and end apart: 4, of which 2 were waited for; matrix products, arithmetic and copies ran while one was open for 6% of the time, Pallas kernels for 0%

commit v1 on v0

v1 whole, which is shorter than its diff:
```python
import functools

import jax
import jax.numpy as jnp
from jax import lax
from jax.experimental import pallas as pl
from jax.experimental.pallas import tpu as pltpu
from jax.sharding import PartitionSpec as P

CAP = 2
K_TOP = 2
CHUNKS = 2
MESH = pl.DeviceIdType.MESH
F32 = jnp.float32
BF16 = jnp.bfloat16
NT = (((1,), (1,)), ((), ()))
TN = (((0,), (0,)), ((), ()))


def kernel(
    n_store, n_pb,
    pick, dest, hid, tgt, gain, head, pin, pout, query,
    out,
    hid_v, tgt_v, gain_v, wide_w, pin_v, pout_v, query_v,
    normed, logits, inner_v, mask_v, dead_v,
    q_rows, q_mid, q_send, q_recv,
    hit_send, hit_recv, u_send, u_recv, g_send, g_recv, g_rows, s_send, s_recv,
    load_sem, hid_sem, head_sem, send_sem, recv_sem,
):
    examples, tokens, width = hid.shape
    cands = pick.shape[0]
    total_tok = cands * tokens
    v_dev = head.shape[1]
    k_in = pin.shape[1]
    m_out = pout.shape[1]
    m_loc = m_out // n_pb
    half = m_loc // 2
    per_query = query.shape[0]
    me_s = lax.axis_index("store")
    me_p = lax.axis_index("pb")

    def pb_peer(i):
        return lax.rem(me_p + i, n_pb)

    def store_peer(i):
        return lax.rem(me_s + i, n_store)

    small = [
        pltpu.make_async_copy(src, dst, load_sem.at[i])
        for i, (src, dst) in enumerate(
            [(gain, gain_v), (tgt, tgt_v), (pout, pout_v), (pin, pin_v), (query, query_v)]
        )
    ]
    gain_load, tgt_load, pout_load, pin_load, query_load = small
    cuts = list(range(0, v_dev, 256)) + [v_dev]
    head_loads = [
        pltpu.make_async_copy(
            head.at[:, lo:hi], wide_w.at[:, lo:hi], head_sem.at[i]
        )
        for i, (lo, hi) in enumerate(zip(cuts[:-1], cuts[1:]))
    ]

    def hid_load(e):
        return pltpu.make_async_copy(hid.at[e], hid_v.at[e], hid_sem.at[e])

    gain_load.start()

    @pl.loop(0, examples)
    def _(e):
        hid_load(e).start()

    tgt_load.start()
    pout_load.start()
    pin_load.start()
    for load in head_loads:
        load.start()
    query_load.start()

    barrier = pltpu.get_barrier_semaphore()
    for i in range(1, n_pb):
        pl.semaphore_signal(barrier, inc=1, device_id={"pb": pb_peer(i)}, device_id_type=MESH)

    @pl.loop(1, n_store)
    def _(i):
        pl.semaphore_signal(
            barrier, inc=1, device_id={"store": store_peer(i)}, device_id_type=MESH
        )

    gain_load.wait()
    rows = 16

    @pl.loop(0, examples)
    def _(e):
        hid_load(e).wait()
        for r in range(0, tokens, rows):
            wide = hid_v[e, r:r + rows, :].astype(F32)
            scale = lax.rsqrt(jnp.mean(wide * wide, axis=1, keepdims=True) + 1e-05)
            wide = hid_v[e, r:r + rows, :].astype(F32)
            normed[e, r:r + rows, :] = (wide * scale * gain_v[...]).astype(BF16)

    pin_load.wait()
    wide_w[:, v_dev:v_dev + k_in] = pin_v[...]
    tgt_load.wait()
    pout_load.wait()
    picks = [pick[c] for c in range(cands)]

    wanted = jnp.concatenate([tgt_v[pl.ds(p, 1), :] for p in picks], axis=1)
    column = lax.broadcasted_iota(jnp.int32, (v_dev, total_tok), 0) + me_p * v_dev
    hit = jnp.where(column == wanted, 1.0, 0.0).astype(BF16)
    hit_rows = lax.dot_general(pout_v[...], hit, TN, preferred_element_type=F32)
    hit_send[...] = hit_rows.astype(BF16).reshape(n_pb, m_loc, total_tok)

    pl.semaphore_wait(barrier, n_pb - 1 + n_store - 1)

    def pb_copy(i, src, dst, kind):
        return pltpu.make_async_remote_copy(
            src_ref=src, dst_ref=dst, send_sem=send_sem.at[kind], recv_sem=recv_sem.at[kind],
            device_id={"pb": pb_peer(i)}, device_id_type=MESH,
        )

    sent = []
    for i in range(1, n_pb):
        copy = pb_copy(i, hit_send.at[pb_peer(i)], hit_recv.at[me_p], 0)
        copy.start()
        sent.append(copy)
    hit_recv[me_p] = hit_send[me_p]

    part_c = cands // CHUNKS
    part_t = part_c * tokens
    cuts = cuts[:-1] + [v_dev + k_in]
    for chunk in range(CHUNKS):
        lo_t = chunk * part_t
        lhs = [normed[p] for p in picks[chunk * part_c:(chunk + 1) * part_c]]
        lhs = jnp.concatenate(lhs, axis=0)
        for n, (lo, hi) in enumerate(zip(cuts[:-1], cuts[1:])):
            if chunk == 0:
                head_loads[n].wait()
            logits[lo_t:lo_t + part_t, lo:hi] = jnp.dot(
                lhs, wide_w[:, lo:hi], preferred_element_type=F32
            )
        local = logits[lo_t:lo_t + part_t, :v_dev]
        top = jnp.max(local, axis=1, keepdims=True)
        expo = jnp.exp(local - top)
        total = jnp.sum(expo, axis=1, keepdims=True)
        part = jnp.dot(expo.astype(BF16), pout_v[...], preferred_element_type=F32)
        lane = lax.broadcasted_iota(jnp.int32, (part_t, 128), 1)
        stats = jnp.where(lane == 0, top, total)
        part_rows = part.T
        stat_rows = stats.T[0:8]
        for p in range(n_pb):
            u_send[chunk, p, 0:m_loc, :] = part_rows[p * m_loc:(p + 1) * m_loc]
            u_send[chunk, p, m_loc:m_loc + 8, :] = stat_rows
        for i in range(1, n_pb):
            copy = pb_copy(i, u_send.at[chunk, pb_peer(i)], u_recv.at[chunk, me_p], 1 + chunk)
            copy.start()
            sent.append(copy)
        u_recv[chunk, me_p] = u_send[chunk, me_p]

    query_load.wait()
    for k in range(k_in):
        q_rows[k * per_query:(k + 1) * per_query, :] = query_v[
            :, k * m_out:(k + 1) * m_out
        ].astype(F32)
    low = lax.broadcasted_iota(jnp.int32, (half, 2 * k_in), 1) < k_in
    for q in range(per_query):
        square = q_rows[pl.ds(q, k_in, stride=per_query), :]
        turned = jnp.concatenate([square, square], axis=0).T
        for p in range(n_pb):
            first = turned[p * m_loc:p * m_loc + half]
            second = turned[p * m_loc + half:(p + 1) * m_loc]
            q_mid[pl.ds(p * half * per_query + q, half, stride=per_query), :] = jnp.where(
                low, first, second
            )
    q_send[...] = q_mid[...].astype(BF16).reshape(q_send.shape)
    q_kind = 1 + CHUNKS
    for i in range(1, n_pb):
        copy = pb_copy(i, q_send.at[pb_peer(i)], q_recv.at[me_p], q_kind)
        copy.start()
        sent.append(copy)
    q_recv[me_p] = q_send[me_p]

    dests = [dest[c] for c in range(cands)]
    ranks = []
    for c in range(cands):
        rank = jnp.int32(0)
        for d in dests[:c]:
            rank = rank + (d == dests[c]).astype(jnp.int32)
        ranks.append(rank)
    block_of = jnp.concatenate(
        [jnp.full((1, tokens), d, jnp.int32) for d in dests], axis=1
    )
    grid_b = lax.broadcasted_iota(jnp.int32, (n_store * m_loc, total_tok), 0) // m_loc
    mask_v[...] = jnp.where(grid_b == block_of, 1.0, 0.0).astype(BF16)
    rank_of = jnp.concatenate([jnp.full((tokens, 2 * k_in), r, jnp.int32) for r in ranks], axis=0)
    inner = logits[:, v_dev:v_dev + k_in]
    inner = jnp.concatenate([inner, inner], axis=1)
    lane_r = lax.broadcasted_iota(jnp.int32, (total_tok, 2 * k_in), 1) // k_in
    inner = jnp.where(lane_r == rank_of, inner, 0.0)
    inner_hi = inner.astype(BF16)
    inner_v[:, :2 * k_in] = inner_hi
    inner_v[:, 2 * k_in:] = (inner - inner_hi.astype(F32)).astype(BF16)
    row_b = lax.broadcasted_iota(jnp.int32, (n_store * m_loc, 2 * k_in), 0) // m_loc
    row_r = lax.broadcasted_iota(jnp.int32, (n_store * m_loc, 2 * k_in), 1) // k_in
    held = jnp.zeros((n_store * m_loc, 2 * k_in), jnp.int32)
    for d in dests:
        held = held + (row_b == d).astype(jnp.int32)
    dead_v[...] = jnp.where(row_r < held, 0.0, jnp.nan).astype(F32)

    def wait_recv(ref, kind):
        pltpu.make_async_copy(ref, ref, recv_sem.at[kind]).wait()

    wait_recv(hit_recv.at[0:n_pb - 1], 0)
    hit_sum = hit_recv[0].astype(F32)
    for p in range(1, n_pb):
        hit_sum = hit_sum + hit_recv[p].astype(F32)
    outer = []
    for chunk in range(CHUNKS):
        wait_recv(u_recv.at[chunk, 0:n_pb - 1], 1 + chunk)
        tops = [u_recv[chunk, p, m_loc:m_loc + 1, :] for p in range(n_pb)]
        sums = [u_recv[chunk, p, m_loc + 1:m_loc + 2, :] for p in range(n_pb)]
        top = functools.reduce(jnp.maximum, tops)
        weights = [jnp.exp(t - top) for t in tops]
        total = functools.reduce(jnp.add, [w * s for w, s in zip(weights, sums)])
        acc = functools.reduce(
            jnp.add, [w * u_recv[chunk, p, 0:m_loc, :] for p, w in enumerate(weights)]
        )
        outer.append(acc / total - hit_sum[:, chunk * part_t:(chunk + 1) * part_t])
    outer = jnp.concatenate(outer, axis=1)

    outer_hi = outer.astype(BF16)
    outer_lo = (outer - outer_hi.astype(F32)).astype(BF16)
    mask = mask_v[...].reshape(n_store, m_loc, total_tok)
    placed_hi = (mask * outer_hi[None]).reshape(n_store * m_loc, total_tok)
    placed_lo = (mask * outer_lo[None]).reshape(n_store * m_loc, total_tok)
    both = jnp.dot(placed_hi, inner_v[...], preferred_element_type=F32)
    rest = jnp.dot(placed_lo, inner_v[:, :2 * k_in], preferred_element_type=F32)
    grads = both[:, :2 * k_in] + (both[:, 2 * k_in:] + rest) + dead_v[...]
    g_send[...] = grads.astype(BF16).reshape(g_send.shape)
    g_kind = 2 + CHUNKS

    def g_copy(i):
        peer = store_peer(i)
        return pltpu.make_async_remote_copy(
            src_ref=g_send.at[peer], dst_ref=g_recv.at[me_s],
            send_sem=send_sem.at[g_kind], recv_sem=recv_sem.at[g_kind],
            device_id={"store": peer}, device_id_type=MESH,
        )

    @pl.loop(1, n_store)
    def _(i):
        g_copy(i).start()

    g_recv[me_s] = g_send[me_s]
    wait_recv(q_recv.at[0:n_pb - 1], q_kind)
    lhs = jnp.concatenate(
        [q_recv[:, j].reshape(n_pb * per_query, 2 * k_in) for j in range(half)], axis=1
    )
    wait_recv(g_recv.at[0:n_store - 1], g_kind)

    g_rows[...] = g_recv[...].astype(F32).reshape(g_rows.shape)
    low = lax.broadcasted_iota(jnp.int32, (n_store, 2 * k_in), 1) < k_in
    rhs = []
    for j in range(half):
        first = g_rows[pl.ds(j, n_store, stride=m_loc), :]
        second = g_rows[pl.ds(j + half, n_store, stride=m_loc), :]
        slot0 = jnp.where(low, first, pltpu.roll(second, k_in, 1))
        slot1 = jnp.where(low, pltpu.roll(first, k_in, 1), second)
        rhs.append(jnp.concatenate([slot0, slot1], axis=0))
    rhs = jnp.concatenate(rhs, axis=1).astype(BF16)
    part = lax.dot_general(lhs, rhs, NT, preferred_element_type=F32)
    slots = CAP * n_store
    s_send[...] = part.reshape(n_pb, per_query, slots)
    s_kind = 3 + CHUNKS
    for i in range(1, n_pb):
        copy = pb_copy(i, s_send.at[pb_peer(i)], s_recv.at[me_p], s_kind)
        copy.start()
        sent.append(copy)
    s_recv[me_p] = s_send[me_p]
    wait_recv(s_recv.at[0:n_pb - 1], s_kind)

    scores = s_recv[0]
    for p in range(1, n_pb):
        scores = scores + s_recv[p]
    scores = jnp.where(scores == scores, scores, jnp.float32(-1e30))
    lane = lax.broadcasted_iota(jnp.int32, scores.shape, 1)
    best = jnp.max(scores, axis=1, keepdims=True)
    at = jnp.min(jnp.where(scores == best, lane, slots), axis=1, keepdims=True)
    second = jnp.max(jnp.where(lane == at, jnp.float32(-3e38), scores), axis=1, keepdims=True)
    out[...] = jnp.where(
        lax.broadcasted_iota(jnp.int32, (per_query, K_TOP), 1) == 0, best, second
    )

    for copy in sent:
        copy.wait_send()

    @pl.loop(1, n_store)
    def _(i):
        g_copy(i).wait_send()


def shards(n_store, n_pb, stored_hidden, targets, pick, dest, norm_gain, head, proj_in, proj_out,
           query_grads):
    examples, tokens, width = stored_hidden.shape
    cands = pick.shape[0]
    total = cands * tokens
    v_dev = head.shape[1]
    k_in = proj_in.shape[1]
    m_out = proj_out.shape[1]
    m_loc = m_out // n_pb
    half = m_loc // 2
    per_query = query_grads.shape[0]
    part_t = total // CHUNKS
    wide_n = v_dev + k_in
    slots = CAP * n_store
    any_spec = pl.BlockSpec(memory_space=pl.ANY)
    smem = pl.BlockSpec(memory_space=pltpu.SMEM)
    vmem = pltpu.VMEM
    kinds = 4 + CHUNKS
    return pl.pallas_call(
        functools.partial(kernel, n_store, n_pb),
        out_shape=jax.ShapeDtypeStruct((per_query, K_TOP), F32),
        in_specs=[smem, smem] + [any_spec] * 7,
        out_specs=pl.BlockSpec(memory_space=pltpu.VMEM),
        scratch_shapes=[
            vmem((examples, tokens, width), BF16),
            vmem((examples, tokens), jnp.int32),
            vmem((1, width), F32),
            vmem((width, wide_n), BF16),
            vmem((width, k_in), BF16),
            vmem((v_dev, m_out), BF16),
            vmem((per_query, k_in * m_out), BF16),
            vmem((examples, tokens, width), BF16),
            vmem((total, wide_n), F32),
            vmem((total, 4 * k_in), BF16),
            vmem((n_store * m_loc, total), BF16),
            vmem((n_store * m_loc, 2 * k_in), F32),
            vmem((k_in * per_query, m_out), F32),
            vmem((n_pb * half * per_query, 2 * k_in), F32),
            vmem((n_pb, half, per_query, 2 * k_in), BF16),
            vmem((n_pb, half, per_query, 2 * k_in), BF16),
            vmem((n_pb, m_loc, total), BF16),
            vmem((n_pb, m_loc, total), BF16),
            vmem((CHUNKS, n_pb, m_loc + 8, part_t), F32),
            vmem((CHUNKS, n_pb, m_loc + 8, part_t), F32),
            vmem((n_store, m_loc, 2 * k_in), BF16),
            vmem((n_store, m_loc, 2 * k_in), BF16),
            vmem((n_store * m_loc, 2 * k_in), F32),
            vmem((n_pb, per_query, slots), F32),
            vmem((n_pb, per_query, slots), F32),
            pltpu.SemaphoreType.DMA((5,)),
            pltpu.SemaphoreType.DMA((examples,)),
            pltpu.SemaphoreType.DMA((-(-v_dev // 256),)),
            pltpu.SemaphoreType.DMA((kinds,)),
            pltpu.SemaphoreType.DMA((kinds,)),
        ],
        compiler_params=pltpu.CompilerParams(
            collective_id=0, has_side_effects=True, vmem_limit_bytes=48 * 1024 * 1024
        ),
        name="attribution",
    )(pick, dest, stored_hidden, targets, norm_gain.reshape(1, width), head, proj_in, proj_out,
      query_grads)


def solution(mesh):
    placed = (
        P("store", None, None),
        P("store", None),
        P("store"),
        P("store"),
        P(),
        P(None, "pb"),
        P(),
        P("pb", None),
        P(("store", "pb"), None),
    )
    body = functools.partial(shards, mesh.shape["store"], mesh.shape["pb"])
    return jax.shard_map(
        body, mesh=mesh, in_specs=placed, out_specs=P(("store", "pb"), None), check_vma=False
    )
```

time: 627 us -> 44.9 us (0.07)
  waiting for transfers between devices: 459 us -> 0 us
  other arithmetic: 44.6 us -> 0 us
  Pallas kernels: 0 us -> 37.9 us
  matrix products: 36.8 us -> 0 us
  starting transfers between devices: 30.7 us -> 0 us
  blocking collectives: 27.2 us -> 0 us
  between operations: 13.6 us -> 0.03 us
  local copies, waits for them, and re-layouts: 13.1 us -> 6.75 us
    all_to_all x3 -> x0, waiting for transfers between devices: 383 us -> none  [the longest x1 383 us: shards(): lax.all_to_all(rows, 'store', split_axis=0, concat_axis=0, tiled=True)]
    psum x1 -> x0, waiting for transfers between devices: 75.8 us -> none  [project_grads(): outer_side = lax.psum(outer_part, 'pb')]
    pallas_call x0 -> x1, Pallas kernels: none -> 37.9 us  [shards(): pl.pallas_call(functools.partial(kernel, n_store, n_pb), out_shape=jax.Sh...]
    dot_general x5 -> x0, matrix products: 36.8 us -> none  [the longest x1 17.8 us: project_grads(): logits = jnp.dot(normed, head, preferred_element_type=jnp.float32)]
    all_to_all x3 -> x0, starting transfers between devices: 30.6 us -> none  [the longest x1 12 us: shards(): lax.all_to_all(live_flag, 'store', split_axis=0, concat_axis=0, tiled=True)]
    all_gather x2 -> x0, blocking collectives: 27.2 us -> none  [combined_all(): gathered = jax.tree.map(lambda a: lax.all_gather(a, axis), part)]
    convert_element_type x2 -> x0, other arithmetic: 15.5 us -> none  [the longest x1 15.5 us: project_grads(): normed = (wide * scale[:, None] * norm_gain[None, :]).astype(jnp.bfloat16)]
    select_n x3 -> x0, other arithmetic: 15.1 us -> none  [the longest x1 14.3 us: shards(): rows = jnp.where(live[:, None, None], rows, jnp.zeros_like(rows))]
  transfers between devices with their start and end apart: 4 -> 0, of which waited for: 2 -> 0; matrix products, arithmetic and copies ran while one was open for 6% -> 0% of each run, Pallas kernels for 0% -> 0%
where the time goes in v1:
time: 44.9 us; the launch traced here: 44.6 us
  Pallas kernels  37.9 us (84%)
  local copies, waits for them, and re-layouts  6.75 us (15%)
    pallas_call x1, Pallas kernels, shards(): pl.pallas_call(functools.partial(kernel, n_store, n_pb), out_shape=jax.Sh...  37.9 us
    unnamed x13, local copies, waits for them, and re-layouts  6.11 us

profile of v1, /device:TPU:1, one launch (start us, length us, event | category | flops | bytes accessed | tf_op | source)
XLA Modules:
  0.0 44.6 jit_solution(2045166007891609811)
XLA Ops:
  0.0 1.5 %copy.10.pin = bf16[4096,64]{1,0:T(8,128)(2,1)S(1)} copy(bf16[4096,64]{0,1:T(8,128)(2,1)} %param.15) | data formatting | bytes 1048576 | tf_op args[6]
  1.5 0.0 copy-start
  1.5 0.9 %copy-done = bf16[16,8192]{1,0:T(8,128)(2,1)S(1)} copy-done((bf16[16,8192]{1,0:T(8,128)(2,1)S(1)}, bf16[16,8192]{1,0:T(8,128)(2,1)}, u32[]{:S(2)}) %copy-start) | copy-done | bytes 262168
  2.5 0.0 copy-start.1
  2.5 0.9 %copy-done.1 = bf16[640,128]{1,0:T(8,128)(2,1)S(1)} copy-done((bf16[640,128]{1,0:T(8,128)(2,1)S(1)}, bf16[640,128]{1,0:T(8,128)(2,1)}, u32[]{:S(2)}) %copy-start.1) | copy-done | bytes 163864
  3.4 0.0 copy-start.2
  3.4 0.7 %copy-done.2 = f32[4096]{0:T(1024)S(1)} copy-done((f32[4096]{0:T(1024)S(1)}, f32[4096]{0:T(1024)}, u32[]{:S(2)}) %copy-start.2) | copy-done | bytes 16408
  4.1 0.0 copy-start.3
  4.1 0.7 %copy-done.3 = s32[20,32]{1,0:T(8,128)S(1)} copy-done((s32[20,32]{1,0:T(8,128)S(1)}, s32[20,32]{1,0:T(8,128)}, u32[]{:S(2)}) %copy-start.3) | copy-done | bytes 2584
  4.8 0.0 copy-start.4
  4.8 0.7 %copy-done.4 = s32[16]{0:T(128)S(1)} copy-done((s32[16]{0:T(128)S(1)}, s32[16]{0:T(128)}, u32[]{:S(2)}) %copy-start.4) | copy-done | bytes 88
  5.5 0.0 copy-start.5
  5.5 0.7 %copy-done.5 = s32[16]{0:T(128)S(1)} copy-done((s32[16]{0:T(128)S(1)}, s32[16]{0:T(128)}, u32[]{:S(2)}) %copy-start.5) | copy-done | bytes 88
  6.1 37.9 %attribution.1 = f32[16,2]{1,0:T(8,128)S(1)} custom-call(s32[16]{0:T(128)S(1)} %copy-done.4, s32[16]{0:T(128)S(1)} %copy-done.5, bf16[20,32,4096]{2,1,0:T(8,128)(2,1)} %hid.1, s32[20,32]{1,0:T(8,128)S(1)} %copy-done.3, f32[1,4096]{1,0:T(1,128)S(1)} %bitcast.1, bf16[4096,640]{1,0:T(8,128)(2,1)} %head.1, bf16[4096,64]{1,0:T(8,128)(2,1)S(1)} %copy.10.pin, ...), custom_call_target="tpu_custom_call" | custom-call | tf_op jit(solution)/shard_map/attribution/pallas_call | solution.py:319
  44.0 0.6 %copy.11 = f32[16,2]{0,1:T(2,128)} copy(f32[16,2]{1,0:T(8,128)S(1)} %attribution.1) | data formatting | bytes 256 | tf_op jit(solution)/shard_map/attribution/pallas_call | solution.py:319
Async XLA Ops:
  1.5 1.0 %copy-start = (bf16[16,8192]{1,0:T(8,128)(2,1)S(1)}, bf16[16,8192]{1,0:T(8,128)(2,1)}, u32[]{:S(2)}) copy-start(bf16[16,8192]{1,0:T(8,128)(2,1)} %query.1) | copy-start | bytes 786436
  2.5 0.9 %copy-start.1 = (bf16[640,128]{1,0:T(8,128)(2,1)S(1)}, bf16[640,128]{1,0:T(8,128)(2,1)}, u32[]{:S(2)}) copy-start(bf16[640,128]{1,0:T(8,128)(2,1)} %pout.1) | copy-start | bytes 491524
  3.4 0.7 %copy-start.2 = (f32[4096]{0:T(1024)S(1)}, f32[4096]{0:T(1024)}, u32[]{:S(2)}) copy-start(f32[4096]{0:T(1024)} %param.13) | copy-start | bytes 49156
  4.1 0.7 %copy-start.3 = (s32[20,32]{1,0:T(8,128)S(1)}, s32[20,32]{1,0:T(8,128)}, u32[]{:S(2)}) copy-start(s32[20,32]{1,0:T(8,128)} %tgt.1) | copy-start | bytes 7684
  4.8 0.7 %copy-start.4 = (s32[16]{0:T(128)S(1)}, s32[16]{0:T(128)}, u32[]{:S(2)}) copy-start(s32[16]{0:T(128)} %pick.1) | copy-start | bytes 196
  5.5 0.7 %copy-start.5 = (s32[16]{0:T(128)S(1)}, s32[16]{0:T(128)}, u32[]{:S(2)}) copy-start(s32[16]{0:T(128)} %dest.1) | copy-start | bytes 196

commit v2 on v1

v2 whole, which is shorter than its diff:
```python
import functools

import jax
import jax.numpy as jnp
from jax import lax
from jax.experimental import pallas as pl
from jax.experimental.pallas import tpu as pltpu
from jax.sharding import PartitionSpec as P

CAP = 2
K_TOP = 2
CHUNKS = 2
STEP = 128
MESH = pl.DeviceIdType.MESH
F32 = jnp.float32
BF16 = jnp.bfloat16
NT = (((1,), (1,)), ((), ()))
TN = (((0,), (0,)), ((), ()))


def ring_hops(i, n):
    y, z = i % 4, i // 4
    return min(y, 4 - y) + max(min(z, n // 4 - z), min(z + 1, n // 4 - z - 1))


def kernel(
    n_store, n_pb,
    pick_h, dest_h, hid, tgt, gain, head, pin, pout, query,
    out,
    pick, dest, hid_v, tgt_v, gain_v, wide_w, pin_v, pout_v, query_v,
    normed, logits, inner_v, mask_v, dead_v, wanted_v,
    q_rows, q_mid, q_send, q_recv,
    hit_send, hit_recv, u_send, u_recv, t_send, t_recv, g_send, g_recv, g_rows, s_send, s_recv,
    load_sem, hid_sem, head_sem, send_sem, recv_sem,
):
    examples, tokens, width = hid.shape
    cands = pick_h.shape[0]
    total_tok = cands * tokens
    v_dev = head.shape[1]
    k_in = pin.shape[0]
    m_out = pout.shape[1]
    m_loc = m_out // n_pb
    half = m_loc // 2
    per_query = query.shape[0]
    me_s = lax.axis_index("store")
    me_p = lax.axis_index("pb")

    def pb_peer(i):
        return lax.rem(me_p + i, n_pb)

    far_pb = sorted(range(1, n_pb), key=lambda i: abs(i - n_pb // 2))

    def store_peer(i):
        return lax.rem(me_s + i, n_store)

    small = [
        pltpu.make_async_copy(src, dst, load_sem.at[i])
        for i, (src, dst) in enumerate(
            [(gain, gain_v), (tgt, tgt_v), (pout, pout_v), (pin, pin_v), (query, query_v),
             (pick_h, pick), (dest_h, dest)]
        )
    ]
    gain_load, tgt_load, pout_load, pin_load, query_load, pick_load, dest_load = small
    cuts = list(range(0, v_dev, 256)) + [v_dev]
    head_loads = [
        pltpu.make_async_copy(
            head.at[:, lo:hi], wide_w.at[:, lo:hi], head_sem.at[i]
        )
        for i, (lo, hi) in enumerate(zip(cuts[:-1], cuts[1:]))
    ]

    def hid_load(e):
        return pltpu.make_async_copy(hid.at[e], hid_v.at[e], hid_sem.at[e])

    for load in (pick_load, dest_load, tgt_load, pout_load, pin_load, gain_load):
        load.start()

    @pl.loop(0, examples)
    def _(e):
        hid_load(e).start()

    head_loads[0].start()

    barrier = pltpu.get_barrier_semaphore()
    for i in range(1, n_pb):
        pl.semaphore_signal(barrier, inc=1, device_id={"pb": pb_peer(i)}, device_id_type=MESH)

    @pl.loop(1, n_store)
    def _(i):
        pl.semaphore_signal(
            barrier, inc=1, device_id={"store": store_peer(i)}, device_id_type=MESH
        )

    for load in (pick_load, dest_load, tgt_load, pout_load, pin_load, gain_load):
        load.wait()
    picks = [pick[c] for c in range(cands)]
    wanted = jnp.concatenate([tgt_v[pl.ds(p, 1), :] for p in picks], axis=1) - me_p * v_dev
    column = lax.broadcasted_iota(jnp.int32, (v_dev, total_tok), 0)
    hit = jnp.where(column == wanted, 1.0, 0.0).astype(BF16)
    hit_rows = lax.dot_general(pout_v[...], hit, TN, preferred_element_type=F32)
    hit_send[...] = hit_rows.astype(BF16).reshape(n_pb, m_loc, total_tok)
    wanted_v[...] = jnp.broadcast_to(wanted.astype(F32), (128, total_tok)).T
    wide_w[:, v_dev:v_dev + k_in] = pin_v[...].T

    def pb_copy(i, src, dst, kind):
        return pltpu.make_async_remote_copy(
            src_ref=src, dst_ref=dst, send_sem=send_sem.at[kind], recv_sem=recv_sem.at[kind],
            device_id={"pb": pb_peer(i)}, device_id_type=MESH,
        )

    def hid_wait(lo, hi):
        pl.loop(lo, hi)(lambda e: hid_load(e).wait())

    hid_wait(0, examples)
    for load in head_loads[1:]:
        load.start()
    query_load.start()

    rows = 16
    step = STEP

    def normalise(lo):
        for t in range(lo, lo + step, rows):
            p, r = picks[t // tokens], t % tokens
            square = jnp.zeros((rows, 128), F32)
            for c in range(0, width, 128):
                wide = hid_v[p, r:r + rows, c:c + 128].astype(F32)
                square = square + wide * wide
            mean = jnp.sum(square, axis=1, keepdims=True) * (1.0 / width)
            scale = jnp.broadcast_to(lax.rsqrt(mean + 1e-05), (rows, 128))
            for c in range(0, width, 128):
                wide = hid_v[p, r:r + rows, c:c + 128].astype(F32)
                normed[t:t + rows, c:c + 128] = (wide * scale * gain_v[:, c:c + 128]).astype(BF16)

    def multiply(lo, n):
        c0, c1 = cuts[n], cuts[n + 1]
        logits[lo:lo + step, c0:c1] = jnp.dot(
            normed[lo:lo + step, :], wide_w[:, c0:c1], preferred_element_type=F32
        )

    cuts = cuts[:-1] + [v_dev + k_in]
    last = len(cuts) - 2
    normalise(0)
    for n in range(last):
        head_loads[n].wait()
        if n == last - 1:
            pl.semaphore_wait(barrier, n_pb - 1 + n_store - 1)
            for i in far_pb:
                copy = pb_copy(i, hit_send.at[pb_peer(i)], hit_recv.at[me_p], 0)
                copy.start()
            hit_recv[me_p] = hit_send[me_p]
        for lo in range(0, total_tok, step):
            multiply(lo, n)
            if n == 0 and lo + step < total_tok:
                normalise(lo + step)
    head_loads[last].wait()
    for lo in range(0, total_tok, step):
        multiply(lo, last)

    part_t = total_tok // CHUNKS
    subs = part_t // step
    lane = lax.broadcasted_iota(jnp.int32, (step, 128), 1)
    entry = lax.broadcasted_iota(jnp.int32, (step, v_dev), 1).astype(F32)
    t_send[...] = jnp.zeros(t_send.shape, F32)
    for chunk in range(CHUNKS):
        for sub in range(subs):
            lo = chunk * part_t + sub * step
            local = logits[lo:lo + step, :v_dev]
            top = jnp.max(local, axis=1, keepdims=True)
            expo = jnp.exp(local - top)
            target = jnp.concatenate([wanted_v[lo:lo + step, :]] * (v_dev // 128), axis=1)
            is_hit = entry == target
            others = jnp.where(is_hit, 0.0, expo)
            total = jnp.sum(others, axis=1, keepdims=True)
            own = jnp.sum(jnp.where(is_hit, expo, 0.0), axis=1, keepdims=True)
            part = jnp.dot(others.astype(BF16), pout_v[...], preferred_element_type=F32)
            stats = jnp.where(lane == 0, top, jnp.where(lane == 1, total, own)).T
            for row in range(3):
                t_send[chunk, row * subs + sub:row * subs + sub + 1, :] = stats[row:row + 1]
            u_send[chunk, :, :, sub * step:(sub + 1) * step] = part.T.astype(BF16).reshape(
                n_pb, m_loc, step
            )
        for i in far_pb:
            copy = pb_copy(i, u_send.at[chunk, pb_peer(i)], u_recv.at[chunk, me_p], 1 + 2 * chunk)
            copy.start()
            copy = pb_copy(i, t_send.at[chunk], t_recv.at[chunk, me_p], 2 + 2 * chunk)
            copy.start()
        u_recv[chunk, me_p] = u_send[chunk, me_p]
        t_recv[chunk, me_p] = t_send[chunk]

    query_load.wait()
    for k in range(k_in):
        q_rows[k * per_query:(k + 1) * per_query, :] = query_v[
            :, k * m_out:(k + 1) * m_out
        ].astype(F32)
    low = lax.broadcasted_iota(jnp.int32, (half, 2 * k_in), 1) < k_in
    for q in range(per_query):
        square = q_rows[pl.ds(q, k_in, stride=per_query), :]
        turned = jnp.concatenate([square, square], axis=0).T
        for p in range(n_pb):
            first = turned[p * m_loc:p * m_loc + half]
            second = turned[p * m_loc + half:(p + 1) * m_loc]
            q_mid[pl.ds(p * half * per_query + q, half, stride=per_query), :] = jnp.where(
                low, first, second
            )
    q_send[...] = q_mid[...].astype(BF16).reshape(q_send.shape)
    q_kind = 1 + 2 * CHUNKS
    q_recv[me_p] = q_send[me_p]

    dests = [dest[c] for c in range(cands)]
    ranks = []
    for c in range(cands):
        rank = jnp.int32(0)
        for d in dests[:c]:
            rank = rank + (d == dests[c]).astype(jnp.int32)
        ranks.append(rank)
    block_of = jnp.concatenate(
        [jnp.full((1, tokens), d, jnp.int32) for d in dests], axis=1
    )
    grid_b = lax.broadcasted_iota(jnp.int32, (n_store * m_loc, total_tok), 0) // m_loc
    mask_v[...] = jnp.where(grid_b == block_of, 1.0, 0.0).astype(BF16)
    rank_of = jnp.concatenate([jnp.full((tokens, 2 * k_in), r, jnp.int32) for r in ranks], axis=0)
    inner = logits[:, v_dev:v_dev + k_in]
    inner = jnp.concatenate([inner, inner], axis=1)
    lane_r = lax.broadcasted_iota(jnp.int32, (total_tok, 2 * k_in), 1) // k_in
    inner = jnp.where(lane_r == rank_of, inner, 0.0)
    inner_hi = inner.astype(BF16)
    inner_v[:, :2 * k_in] = inner_hi
    inner_v[:, 2 * k_in:] = (inner - inner_hi.astype(F32)).astype(BF16)
    row_b = lax.broadcasted_iota(jnp.int32, (n_store * m_loc, 2 * k_in), 0) // m_loc
    row_r = lax.broadcasted_iota(jnp.int32, (n_store * m_loc, 2 * k_in), 1) // k_in
    held = jnp.zeros((n_store * m_loc, 2 * k_in), jnp.int32)
    for d in dests:
        held = held + (row_b == d).astype(jnp.int32)
    dead_v[...] = jnp.where(row_r < held, 0.0, jnp.nan).astype(F32)

    def wait_recv(ref, kind):
        pltpu.make_async_copy(ref, ref, recv_sem.at[kind]).wait()

    def wait_send(ref, kind):
        pltpu.make_async_copy(ref, ref, send_sem.at[kind]).wait()

    wait_recv(hit_recv.at[0:n_pb - 1], 0)
    hit_sum = hit_recv[0].astype(F32)
    for p in range(1, n_pb):
        hit_sum = hit_sum + hit_recv[p].astype(F32)
    for chunk in range(CHUNKS):
        wait_recv(u_recv.at[chunk, 0:n_pb - 1], 1 + 2 * chunk)
        wait_recv(t_recv.at[chunk, 0:n_pb - 1], 2 + 2 * chunk)
    for i in far_pb:
        copy = pb_copy(i, q_send.at[pb_peer(i)], q_recv.at[me_p], q_kind)
        copy.start()
    outer = []
    for chunk in range(CHUNKS):
        for sub in range(subs):
            tops, totals, owns = (
                [t_recv[chunk, p, row * subs + sub:row * subs + sub + 1, :] for p in range(n_pb)]
                for row in range(3)
            )
            top = functools.reduce(jnp.maximum, tops)
            weights = [jnp.exp(t - top) for t in tops]
            others = functools.reduce(jnp.add, [w * t for w, t in zip(weights, totals)])
            total = others + functools.reduce(jnp.add, [w * o for w, o in zip(weights, owns)])
            acc = functools.reduce(jnp.add, [
                w * u_recv[chunk, p, :, sub * step:(sub + 1) * step].astype(F32)
                for p, w in enumerate(weights)
            ])
            lo = chunk * part_t + sub * step
            outer.append((acc - others * hit_sum[:, lo:lo + step]) / total)
    outer = jnp.concatenate(outer, axis=1)

    outer_hi = outer.astype(BF16)
    outer_lo = (outer - outer_hi.astype(F32)).astype(BF16)
    mask = mask_v[...].reshape(n_store, m_loc, total_tok)
    placed_hi = (mask * outer_hi[None]).reshape(n_store * m_loc, total_tok)
    placed_lo = (mask * outer_lo[None]).reshape(n_store * m_loc, total_tok)
    both = jnp.dot(placed_hi, inner_v[...], preferred_element_type=F32)
    rest = jnp.dot(placed_lo, inner_v[:, :2 * k_in], preferred_element_type=F32)
    grads = both[:, :2 * k_in] + (both[:, 2 * k_in:] + rest) + dead_v[...]
    g_send[...] = grads.astype(BF16).reshape(g_send.shape)
    g_kind = 2 + 2 * CHUNKS

    far = sorted(range(1, n_store), key=lambda i: -ring_hops(i, n_store))
    for i in far:
        peer = store_peer(i)
        copy = pltpu.make_async_remote_copy(
            src_ref=g_send.at[peer], dst_ref=g_recv.at[me_s],
            send_sem=send_sem.at[g_kind], recv_sem=recv_sem.at[g_kind],
            device_id={"store": peer}, device_id_type=MESH,
        )
        copy.start()
    g_recv[me_s] = g_send[me_s]
    wait_recv(q_recv.at[0:n_pb - 1], q_kind)
    lhs = jnp.concatenate(
        [q_recv[:, j].reshape(n_pb * per_query, 2 * k_in) for j in range(half)], axis=1
    )
    wait_send(hit_send.at[0:n_pb - 1], 0)
    for chunk in range(CHUNKS):
        wait_send(u_send.at[chunk, 0:n_pb - 1], 1 + 2 * chunk)
        wait_send(t_recv.at[chunk, 0:n_pb - 1], 2 + 2 * chunk)
    wait_send(q_send.at[0:n_pb - 1], q_kind)
    wait_recv(g_recv.at[0:n_store - 1], g_kind)

    g_rows[...] = g_recv[...].astype(F32).reshape(g_rows.shape)
    low = lax.broadcasted_iota(jnp.int32, (n_store, 2 * k_in), 1) < k_in
    rhs = []
    for j in range(half):
        first = g_rows[pl.ds(j, n_store, stride=m_loc), :]
        second = g_rows[pl.ds(j + half, n_store, stride=m_loc), :]
        slot0 = jnp.where(low, first, pltpu.roll(second, k_in, 1))
        slot1 = jnp.where(low, pltpu.roll(first, k_in, 1), second)
        rhs.append(jnp.concatenate([slot0, slot1], axis=0))
    rhs = jnp.concatenate(rhs, axis=1).astype(BF16)
    part = lax.dot_general(lhs, rhs, NT, preferred_element_type=F32)
    slots = CAP * n_store
    s_send[...] = part.reshape(n_pb, per_query, slots)
    s_kind = 3 + 2 * CHUNKS
    for i in far_pb:
        copy = pb_copy(i, s_send.at[pb_peer(i)], s_recv.at[me_p], s_kind)
        copy.start()
    s_recv[me_p] = s_send[me_p]
    wait_send(g_send.at[0:n_store - 1], g_kind)
    wait_recv(s_recv.at[0:n_pb - 1], s_kind)

    scores = s_recv[0]
    for p in range(1, n_pb):
        scores = scores + s_recv[p]
    scores = jnp.where(scores == scores, scores, jnp.float32(-1e30))
    lane = lax.broadcasted_iota(jnp.int32, scores.shape, 1)
    best = jnp.max(scores, axis=1, keepdims=True)
    at = jnp.min(jnp.where(scores == best, lane, slots), axis=1, keepdims=True)
    second = jnp.max(jnp.where(lane == at, jnp.float32(-3e38), scores), axis=1, keepdims=True)
    both = jnp.where(lax.broadcasted_iota(jnp.int32, (per_query, 128), 1) == 0, best, second)
    out[...] = both.T[0:K_TOP]

    wait_send(s_send.at[0:n_pb - 1], s_kind)


def shards(n_store, n_pb, stored_hidden, targets, pick, dest, norm_gain, head, proj_in, proj_out,
           query_grads):
    examples, tokens, width = stored_hidden.shape
    cands = pick.shape[0]
    total = cands * tokens
    v_dev = head.shape[1]
    k_in = proj_in.shape[1]
    m_out = proj_out.shape[1]
    m_loc = m_out // n_pb
    half = m_loc // 2
    per_query = query_grads.shape[0]
    part_t = total // CHUNKS
    wide_n = v_dev + k_in
    slots = CAP * n_store
    any_spec = pl.BlockSpec(memory_space=pl.ANY)
    vmem = pltpu.VMEM
    kinds = 4 + 2 * CHUNKS
    return pl.pallas_call(
        functools.partial(kernel, n_store, n_pb),
        out_shape=jax.ShapeDtypeStruct((K_TOP, per_query), F32),
        in_specs=[any_spec] * 9,
        out_specs=pl.BlockSpec(memory_space=pltpu.VMEM),
        scratch_shapes=[
            pltpu.SMEM((cands,), jnp.int32),
            pltpu.SMEM((cands,), jnp.int32),
            vmem((examples, tokens, width), BF16),
            vmem((examples, tokens), jnp.int32),
            vmem((1, width), F32),
            vmem((width, wide_n), BF16),
            vmem((k_in, width), BF16),
            vmem((v_dev, m_out), BF16),
            vmem((per_query, k_in * m_out), BF16),
            vmem((total, width), BF16),
            vmem((total, wide_n), F32),
            vmem((total, 4 * k_in), BF16),
            vmem((n_store * m_loc, total), BF16),
            vmem((n_store * m_loc, 2 * k_in), F32),
            vmem((total, 128), F32),
            vmem((k_in * per_query, m_out), F32),
            vmem((n_pb * half * per_query, 2 * k_in), F32),
            vmem((n_pb, half, per_query, 2 * k_in), BF16),
            vmem((n_pb, half, per_query, 2 * k_in), BF16),
            vmem((n_pb, m_loc, total), BF16),
            vmem((n_pb, m_loc, total), BF16),
            vmem((CHUNKS, n_pb, m_loc, part_t), BF16),
            vmem((CHUNKS, n_pb, m_loc, part_t), BF16),
            vmem((CHUNKS, 8, 128), F32),
            vmem((CHUNKS, n_pb, 8, 128), F32),
            vmem((n_store, m_loc, 2 * k_in), BF16),
            vmem((n_store, m_loc, 2 * k_in), BF16),
            vmem((n_store * m_loc, 2 * k_in), F32),
            vmem((n_pb, per_query, slots), F32),
            vmem((n_pb, per_query, slots), F32),
            pltpu.SemaphoreType.DMA((7,)),
            pltpu.SemaphoreType.DMA((examples,)),
            pltpu.SemaphoreType.DMA((-(-v_dev // 256),)),
            pltpu.SemaphoreType.DMA((kinds,)),
            pltpu.SemaphoreType.DMA((kinds,)),
        ],
        compiler_params=pltpu.CompilerParams(
            collective_id=0, has_side_effects=True, vmem_limit_bytes=63 * 1024 * 1024
        ),
        name="attribution",
    )(pick, dest, stored_hidden, targets, norm_gain.reshape(1, width), head, proj_in.T, proj_out,
      query_grads).T


def solution(mesh):
    placed = (
        P("store", None, None),
        P("store", None),
        P("store"),
        P("store"),
        P(),
        P(None, "pb"),
        P(),
        P("pb", None),
        P(("store", "pb"), None),
    )
    body = functools.partial(shards, mesh.shape["store"], mesh.shape["pb"])
    return jax.shard_map(
        body, mesh=mesh, in_specs=placed, out_specs=P(("store", "pb"), None), check_vma=False
    )
```

time: 44.9 us -> 33.7 us (0.75)
  local copies, waits for them, and re-layouts: 6.75 us -> 1.24 us
  Pallas kernels: 37.9 us -> 32.4 us
    pallas_call x1, Pallas kernels: 37.9 us -> 32.4 us  [shards(): pl.pallas_call(functools.partial(kernel, n_store, n_pb), out_shape=jax.Sh...]
    unnamed x13 -> x1, local copies, waits for them, and re-layouts: 6.11 us -> 1.24 us
    pallas_call x1 -> x0, local copies, waits for them, and re-layouts: 0.64 us -> none  [shards(): pl.pallas_call(functools.partial(kernel, n_store, n_pb), out_shape=jax.Sh...]
where the time goes in v2:
time: 33.7 us; the launch traced here: 33.6 us
  Pallas kernels  32.4 us (96%)
  local copies, waits for them, and re-layouts  1.24 us (4%)
    pallas_call x1, Pallas kernels, shards(): pl.pallas_call(functools.partial(kernel, n_store, n_pb), out_shape=jax.Sh...  32.4 us
    unnamed x1, local copies, waits for them, and re-layouts  1.24 us

profile of v2, /device:TPU:1, one launch (start us, length us, event | category | flops | bytes accessed | tf_op | source)
XLA Modules:
  0.0 33.6 jit_solution(1475634923829282470)
XLA Ops:
  0.0 32.4 %attribution.1 = f32[2,16]{1,0:T(2,128)} custom-call(s32[16]{0:T(128)} %pick_h.1, s32[16]{0:T(128)} %dest_h.1, bf16[20,32,4096]{2,1,0:T(8,128)(2,1)} %hid.1, s32[20,32]{1,0:T(8,128)} %tgt.1, f32[1,4096]{1,0:T(1,128)} %bitcast.4, bf16[4096,640]{1,0:T(8,128)(2,1)} %head.1, bf16[64,4096]{1,0:T(8,128)(2,1)} %bitcast.3, bf16[640,128]{1,0:T(8,128)(2,1)} %pout.1, ...), custom_call_target="tpu_custom_call" | custom-call | tf_op jit(solution)/shard_map/attribution/pallas_call | solution.py:356
  32.4 1.2 %copy.11 = f32[16,2]{0,1:T(2,128)} copy(f32[16,2]{0,1:T(2,128)} %bitcast.5) | data formatting | bytes 256
